TPU v7x, 32 devices: a whole 2x2x4 slice. The times are simulated.
32 devices in a mesh: gx: 4 (over y, core), gy: 2 (over x), gz: 4 (over z).
Axes of the slice: x: 2, y: 2, z: 4, core: 2. Of those that a mesh axis runs over, the one named last changes fastest.
Arguments:
- positions: float32 [4, 2, 4, 3, 1024], P('gx', 'gy', 'gz'), may hold values from 0 to 1
- types: int32 [4, 2, 4, 1024], P('gx', 'gy', 'gz'), may hold values from 0 to 3
- tile_lists: int32 [8, 36], replicated, may hold values from 0 to 215, as said below
- hardness: float32 [4], replicated, may hold values from 2 to 8
- electroneg: float32 [4], replicated, may hold values from 2 to 8
- gamma_table: float32 [4], replicated, may hold values from 0.25 to 1
Outputs:
- charges: float32 [4, 2, 4, 1024], P('gx', 'gy', 'gz')
- solutions: float32 [4, 2, 4, 2, 1024], P('gx', 'gy', 'gz')
Inputs may be any that keep to these rules, and one draw needn't show every extreme that they name: `tile_lists`: entry (t, o, u) stands in tile t's list as often as entry (u, 26 - o, t) stands in tile u's list; every offset o of 0 to 26 occurs; the lists are the same for every box.
All inputs are finite; a program needn't handle non-finite values.
Results may differ from a plain program's by a relative error of at most 0.0003.
Values sent between devices are 32-bit elements; how exact they have to be, the bound alone decides.
A program may use at most 64 MiB of HBM per device.

v0:
```python
import jax
import jax.numpy as jnp
from jax import lax
from jax.sharding import PartitionSpec as P

ITERS = 4


CUTOFF = 10.0
COULOMB = 0.3
VOLUME = 10.0


def padded(cells, sides, width):
    for axis, dim in sides:
        count = lax.axis_size(axis)
        ends = count - 1
        head = lax.slice_in_dim(cells, 0, width, axis=dim)
        tail = lax.slice_in_dim(cells, cells.shape[dim] - width, cells.shape[dim], axis=dim)
        cells = jnp.concatenate(
            [
                lax.ppermute(tail, axis, [(i, (i + 1) % count) for i in range(ends)]),
                cells,
                lax.ppermute(head, axis, [((i + 1) % count, i) for i in range(ends)]),
            ],
            axis=dim,
        )
    return cells


def taper(scaled):
    return scaled**4 * (((20.0 * scaled - 70.0) * scaled + 84.0) * scaled - 35.0) + 1.0


def atom_table(types, table):
    kinds = jnp.arange(table.shape[0], dtype=jnp.int32)
    onehot = (types[..., None] == kinds).astype(jnp.float32)
    return jnp.dot(onehot, table, precision=lax.Precision.HIGHEST)


def arrange(raw, tile_count):
    channels = raw.shape[3]
    tile_width = raw.shape[4] // tile_count
    arranged = jnp.transpose(raw.reshape(27, channels, tile_count, tile_width), (1, 0, 2, 3))
    return arranged.reshape(channels, 27 * tile_count, tile_width)


def tile_blocks(nearby, tile_lists, box_edge):
    tile_count = tile_lists.shape[0]
    tile_width = nearby.shape[2]
    local_data = nearby[:, 13 * tile_count : 14 * tile_count]
    diagonal_mask = jnp.arange(tile_width)[:, None] == jnp.arange(tile_width)[None, :]

    def one_tile(inputs):
        mine_data, entries, tile_index = inputs
        others = nearby[:, entries]
        offset_box = entries // tile_count
        shifts = jnp.stack(
            [offset_box // 9 - 1, offset_box // 3 % 3 - 1, offset_box % 3 - 1]
        ).astype(jnp.float32)
        separation = (
            others[:3, :, None, :] + shifts[:, :, None, None] - mine_data[:3, None, :, None]
        ) * box_edge
        spacing = jnp.sqrt(jnp.sum(separation * separation, axis=0))
        present = others[4][:, None, :]
        gamma_other = others[3] + (1.0 - others[4])
        inverse_cube = (mine_data[3][None, :, None] * gamma_other[:, None, :]) ** (-1.5)
        shielding = jnp.cbrt(spacing * spacing * spacing + inverse_cube)
        tapered = jnp.where(spacing < CUTOFF, taper(spacing / CUTOFF), 0.0)
        coupling = COULOMB * tapered / shielding * present
        itself = (entries == 13 * tile_count + tile_index)[:, None, None] & diagonal_mask[None]
        return jnp.where(itself, 0.0, coupling)

    mine_all = jnp.transpose(local_data, (1, 0, 2))
    return lax.map(one_tile, (mine_all, tile_lists, jnp.arange(tile_count, dtype=jnp.int32)))


def couple(blocks, nearby_vectors, tile_lists):
    picked = nearby_vectors[:, tile_lists]
    return jnp.einsum("teij,ktej->kti", blocks, picked, precision=lax.Precision.HIGHEST)


def two_products(residual, image):
    return lax.psum(
        (jnp.sum(residual * residual, axis=1), jnp.sum(residual * image, axis=1)),
        ("gx", "gy", "gz"),
    )


def on_device(positions, types, tile_lists, hardness, electroneg, gamma_table):
    atoms = positions.shape[4]
    tile_count = tile_lists.shape[0]
    box_edge = (atoms * VOLUME) ** (1.0 / 3.0)
    kinds = types[0, 0, 0]
    hardness_atom = atom_table(kinds, hardness)
    electro_atom = atom_table(kinds, electroneg)
    gamma_atom = atom_table(kinds, gamma_table)
    present = jnp.ones_like(gamma_atom)
    centre = jnp.concatenate([positions[0, 0, 0], gamma_atom[None], present[None]], axis=0)[
        None, None, None
    ]
    ghost_raw = padded(centre, (("gx", 0), ("gy", 1), ("gz", 2)), 1)
    blocks = tile_blocks(arrange(ghost_raw, tile_count), tile_lists, box_edge)

    def apply(vectors):
        systems = vectors.shape[0]
        first_raw = padded(vectors[None, None, None, :1], (("gx", 0), ("gy", 1), ("gz", 2)), 1)
        second_raw = padded(vectors[None, None, None, 1:], (("gx", 0), ("gy", 1), ("gz", 2)), 1)
        halo_raw = jnp.concatenate([first_raw, second_raw], axis=3)
        coupled = couple(blocks, arrange(halo_raw, tile_count), tile_lists).reshape(systems, atoms)
        return hardness_atom[None] * vectors + coupled

    right = jnp.stack([-electro_atom, -jnp.ones_like(electro_atom)], axis=0)
    solution = jnp.zeros_like(right)
    residual = right
    image = apply(residual)
    norm_now, product = two_products(residual, image)
    alpha = norm_now / product
    direction = residual
    along = image
    for iteration in range(ITERS):
        solution = solution + alpha[:, None] * direction
        residual = residual - alpha[:, None] * along
        if iteration + 1 < ITERS:
            image = apply(residual)
            norm_next, product = two_products(residual, image)
            ratio = norm_next / norm_now
            alpha = norm_next / (product - ratio * norm_next / alpha)
            direction = residual + ratio[:, None] * direction
            along = image + ratio[:, None] * along
            norm_now = norm_next
    sums = lax.psum(jnp.sum(solution, axis=1), ("gx", "gy", "gz"))
    charges = solution[0] - sums[0] / sums[1] * solution[1]
    return (charges[None, None, None], solution[None, None, None])


def solution(mesh):
    in_specs = (P("gx", "gy", "gz", None, None), P("gx", "gy", "gz", None), P(), P(), P(), P())
    out_specs = (P("gx", "gy", "gz", None), P("gx", "gy", "gz", None, None))
    return jax.shard_map(
        on_device, mesh=mesh, in_specs=in_specs, out_specs=out_specs, check_vma=False
    )
```

profile of v0, /device:TPU:0, one launch (start us, length us, event | category | flops | bytes accessed | tf_op | source)
XLA Modules:
  0.0 558.3 jit_solution(3947430371888833300)
XLA Ops:
  2.7 2.4 collective-permute-start.12
  5.0 1.3 collective-permute-start.13
  7.5 5.2 collective-permute-start
  12.6 1.3 collective-permute-start.1
  13.9 4.3 collective-permute-start.6
  20.2 1.3 collective-permute-start.7
  21.5 3.4 collective-permute-start.2
  24.9 1.3 collective-permute-start.3
  26.3 4.5 collective-permute-start.8
  30.8 1.3 collective-permute-start.9
  32.2 3.5 collective-permute-start.4
  37.0 4.5 collective-permute-start.10
  42.9 4.5 collective-permute-start.14
  47.5 1.3 collective-permute-start.15
  50.1 4.1 collective-permute-done.15
  54.3 4.3 collective-permute-start.16
  58.6 1.5 collective-permute-start.17
  60.2 2.1 gather_fusion.1
  62.4 1.3 collective-permute-done.16
  63.7 4.1 collective-permute-done.17
  68.4 92.8 %while.14 = (s32[]{:T(128)}, f32[8,36,128,128]{3,2,1,0:T(8,128)}, s32[8,36]{1,0:T(8,128)}, s32[8]{0:T(128)S(1)}, f32[5,216,128]{2,0,1:T(8,128)S(1)}, /*index=5*/f32[8,5,128]{2,1,0:T(8,128)S(1)}, s32[]{:T(128)}, s32[1]{0:T(128)}) while((s32[]{:T(128)}, f32[8,36,128,128]{3,2,1,0:T(8,128)}, s32[8,36]{1,0:T(8,128)}, s32[8]{0:T(128)S(1)}, ...), condition=%wide.region_4.5_spmd.clone, body=%wide.region_2.4_spmd.clone.sunk | while | flops 19506696 | bytes 7794025 | solution.py:75
  73.9 6.1 %fusion.73 = f32[8,36,128,128]{3,2,1,0:T(8,128)} fusion(f32[8,36,128,128]{3,2,1,0:T(8,128)} %get-tuple-element.283, s32[]{:T(128)} %get-tuple-element.282, f32[36,128,128]{2,1,0:T(8,128)S(1)} %multiply_reduce_fusion.7, f32[36,128]{1,0:T(8,128)S(1)} %bitcast.203, f32[36,128]{1,0:T(8,128)S(1)} %bitcast_add_fusion.2, f32[128]{0:T(128)S(1)} %slice_bitcast_fusion.12, ...), kind=kLoop, calls=%fused_computation.13.clone.1 | loop fusion | flops 12976128 | bytes 4772900 | tf_op jit(solution)/shard_map/while/body/jit(dynamic_update_index_in_dim)/dynamic_update_slice | solution.py:75
  85.5 6.1 %fusion.73 = f32[8,36,128,128]{3,2,1,0:T(8,128)} fusion(f32[8,36,128,128]{3,2,1,0:T(8,128)} %get-tuple-element.283, s32[]{:T(128)} %get-tuple-element.282, f32[36,128,128]{2,1,0:T(8,128)S(1)} %multiply_reduce_fusion.7, f32[36,128]{1,0:T(8,128)S(1)} %bitcast.203, f32[36,128]{1,0:T(8,128)S(1)} %bitcast_add_fusion.2, f32[128]{0:T(128)S(1)} %slice_bitcast_fusion.12, ...), kind=kLoop, calls=%fused_computation.13.clone.1 | loop fusion | flops 12976128 | bytes 4772900 | tf_op jit(solution)/shard_map/while/body/jit(dynamic_update_index_in_dim)/dynamic_update_slice | solution.py:75
  97.1 6.1 %fusion.73 = f32[8,36,128,128]{3,2,1,0:T(8,128)} fusion(f32[8,36,128,128]{3,2,1,0:T(8,128)} %get-tuple-element.283, s32[]{:T(128)} %get-tuple-element.282, f32[36,128,128]{2,1,0:T(8,128)S(1)} %multiply_reduce_fusion.7, f32[36,128]{1,0:T(8,128)S(1)} %bitcast.203, f32[36,128]{1,0:T(8,128)S(1)} %bitcast_add_fusion.2, f32[128]{0:T(128)S(1)} %slice_bitcast_fusion.12, ...), kind=kLoop, calls=%fused_computation.13.clone.1 | loop fusion | flops 12976128 | bytes 4772900 | tf_op jit(solution)/shard_map/while/body/jit(dynamic_update_index_in_dim)/dynamic_update_slice | solution.py:75
  108.7 6.2 %fusion.73 = f32[8,36,128,128]{3,2,1,0:T(8,128)} fusion(f32[8,36,128,128]{3,2,1,0:T(8,128)} %get-tuple-element.283, s32[]{:T(128)} %get-tuple-element.282, f32[36,128,128]{2,1,0:T(8,128)S(1)} %multiply_reduce_fusion.7, f32[36,128]{1,0:T(8,128)S(1)} %bitcast.203, f32[36,128]{1,0:T(8,128)S(1)} %bitcast_add_fusion.2, f32[128]{0:T(128)S(1)} %slice_bitcast_fusion.12, ...), kind=kLoop, calls=%fused_computation.13.clone.1 | loop fusion | flops 12976128 | bytes 4772900 | tf_op jit(solution)/shard_map/while/body/jit(dynamic_update_index_in_dim)/dynamic_update_slice | solution.py:75
  120.4 6.1 %fusion.73 = f32[8,36,128,128]{3,2,1,0:T(8,128)} fusion(f32[8,36,128,128]{3,2,1,0:T(8,128)} %get-tuple-element.283, s32[]{:T(128)} %get-tuple-element.282, f32[36,128,128]{2,1,0:T(8,128)S(1)} %multiply_reduce_fusion.7, f32[36,128]{1,0:T(8,128)S(1)} %bitcast.203, f32[36,128]{1,0:T(8,128)S(1)} %bitcast_add_fusion.2, f32[128]{0:T(128)S(1)} %slice_bitcast_fusion.12, ...), kind=kLoop, calls=%fused_computation.13.clone.1 | loop fusion | flops 12976128 | bytes 4772900 | tf_op jit(solution)/shard_map/while/body/jit(dynamic_update_index_in_dim)/dynamic_update_slice | solution.py:75
  131.9 6.1 %fusion.73 = f32[8,36,128,128]{3,2,1,0:T(8,128)} fusion(f32[8,36,128,128]{3,2,1,0:T(8,128)} %get-tuple-element.283, s32[]{:T(128)} %get-tuple-element.282, f32[36,128,128]{2,1,0:T(8,128)S(1)} %multiply_reduce_fusion.7, f32[36,128]{1,0:T(8,128)S(1)} %bitcast.203, f32[36,128]{1,0:T(8,128)S(1)} %bitcast_add_fusion.2, f32[128]{0:T(128)S(1)} %slice_bitcast_fusion.12, ...), kind=kLoop, calls=%fused_computation.13.clone.1 | loop fusion | flops 12976128 | bytes 4772900 | tf_op jit(solution)/shard_map/while/body/jit(dynamic_update_index_in_dim)/dynamic_update_slice | solution.py:75
  143.5 6.1 %fusion.73 = f32[8,36,128,128]{3,2,1,0:T(8,128)} fusion(f32[8,36,128,128]{3,2,1,0:T(8,128)} %get-tuple-element.283, s32[]{:T(128)} %get-tuple-element.282, f32[36,128,128]{2,1,0:T(8,128)S(1)} %multiply_reduce_fusion.7, f32[36,128]{1,0:T(8,128)S(1)} %bitcast.203, f32[36,128]{1,0:T(8,128)S(1)} %bitcast_add_fusion.2, f32[128]{0:T(128)S(1)} %slice_bitcast_fusion.12, ...), kind=kLoop, calls=%fused_computation.13.clone.1 | loop fusion | flops 12976128 | bytes 4772900 | tf_op jit(solution)/shard_map/while/body/jit(dynamic_update_index_in_dim)/dynamic_update_slice | solution.py:75
  155.1 6.1 %fusion.73 = f32[8,36,128,128]{3,2,1,0:T(8,128)} fusion(f32[8,36,128,128]{3,2,1,0:T(8,128)} %get-tuple-element.283, s32[]{:T(128)} %get-tuple-element.282, f32[36,128,128]{2,1,0:T(8,128)S(1)} %multiply_reduce_fusion.7, f32[36,128]{1,0:T(8,128)S(1)} %bitcast.203, f32[36,128]{1,0:T(8,128)S(1)} %bitcast_add_fusion.2, f32[128]{0:T(128)S(1)} %slice_bitcast_fusion.12, ...), kind=kLoop, calls=%fused_computation.13.clone.1 | loop fusion | flops 12976128 | bytes 4772900 | tf_op jit(solution)/shard_map/while/body/jit(dynamic_update_index_in_dim)/dynamic_update_slice | solution.py:75
  161.2 18.6 %fusion.36 = (f32[2]{0:T(128)S(1)}, f32[2]{0:T(128)S(1)}, f32[2,1024]{1,0:T(2,128)S(1)}) fusion(f32[1,1024]{1,0:T(1,128)S(1)} %bitcast.217, f32[2,8,36,128]{3,0,2,1:T(2,128)S(1)} %bitcast.204, f32[8,36,128,128]{3,2,1,0:T(8,128)} %get-tuple-element.137, f32[1024]{0:T(1024)S(1)} %bitcast.208), kind=kOutput, calls=%fused_computation.108 | convolution fusion | flops 113258496 | bytes 19185680 | tf_op jit(solution)/shard_map/teij,ktej->kti/dot_general | solution.py:80
  179.8 40.9 %all-reduce.4 = (f32[2]{0:T(128)S(1)}, f32[2]{0:T(128)S(1)}) all-reduce(f32[2]{0:T(128)S(1)} %get-tuple-element.175, f32[2]{0:T(128)S(1)} %get-tuple-element.174), channel_id=1, replica_groups=mesh['gx'=4,'gy'=2,'gz'=4] {'gx','gy','gz'}, use_global_device_ids=true, to_apply=%region_1.2 | all-reduce | flops 4 | bytes 32 | tf_op jit(solution)/shard_map/psum | solution.py:84
  222.1 1.3 collective-permute-start.19
  223.4 5.5 collective-permute-start.24
  230.3 3.9 collective-permute-start.20
  235.5 4.5 collective-permute-start.26
  241.4 2.2 collective-permute-start.22
  243.6 1.3 collective-permute-start.23
  245.7 3.8 collective-permute-start.28
  249.5 1.5 collective-permute-start.29
  251.4 4.1 collective-permute-done.29
  256.0 2.1 gather_fusion.2
  258.2 18.6 %multiply_reduce_fusion.4 = (f32[2]{0:T(128)S(1)}, f32[2]{0:T(128)S(1)}, f32[2,1024]{1,0:T(2,128)S(1)}) fusion(f32[2,1024]{1,0:T(2,128)S(1)} %pad_subtract_fusion, f32[2,8,36,128]{3,0,2,1:T(2,128)S(1)} %bitcast.205, f32[8,36,128,128]{3,2,1,0:T(8,128)} %get-tuple-element.137, f32[1024]{0:T(1024)S(1)} %bitcast.209), kind=kOutput, calls=%fused_computation.119 | convolution fusion | flops 113258496 | bytes 19189776 | tf_op jit(solution)/shard_map/teij,ktej->kti/dot_general | solution.py:80
  276.8 44.0 %all-reduce.3 = (f32[2]{0:T(128)S(1)}, f32[2]{0:T(128)S(1)}) all-reduce(f32[2]{0:T(128)S(1)} %get-tuple-element.173, f32[2]{0:T(128)S(1)} %get-tuple-element.172), channel_id=1, replica_groups=mesh['gx'=4,'gy'=2,'gz'=4] {'gx','gy','gz'}, use_global_device_ids=true, to_apply=%region_8.9 | all-reduce | flops 4 | bytes 32 | tf_op jit(solution)/shard_map/psum | solution.py:84
  323.5 5.5 collective-permute-start.36
  330.3 2.0 collective-permute-start.32
  333.7 4.5 collective-permute-start.38
  339.6 2.1 collective-permute-start.34
  343.9 3.8 collective-permute-start.40
  347.7 1.6 collective-permute-start.41
  349.5 4.1 collective-permute-done.41
  354.2 2.1 gather_fusion.3
  356.3 18.6 %multiply_reduce_fusion.2 = (f32[2]{0:T(128)S(1)}, f32[2]{0:T(128)S(1)}, f32[2,1024]{1,0:T(2,128)S(1)}) fusion(f32[2,1024]{1,0:T(2,128)S(1)} %multiply_subtract_fusion.1, f32[2,8,36,128]{3,0,2,1:T(2,128)S(1)} %bitcast.206, f32[8,36,128,128]{3,2,1,0:T(8,128)} %get-tuple-element.137, f32[1024]{0:T(1024)S(1)} %bitcast.210), kind=kOutput, calls=%fused_computation.115 | convolution fusion | flops 113258496 | bytes 19189776 | tf_op jit(solution)/shard_map/teij,ktej->kti/dot_general | solution.py:80
  374.9 44.0 %all-reduce.2 = (f32[2]{0:T(128)S(1)}, f32[2]{0:T(128)S(1)}) all-reduce(f32[2]{0:T(128)S(1)} %get-tuple-element.171, f32[2]{0:T(128)S(1)} %get-tuple-element.170), channel_id=1, replica_groups=mesh['gx'=4,'gy'=2,'gz'=4] {'gx','gy','gz'}, use_global_device_ids=true, to_apply=%region_12.13 | all-reduce | flops 4 | bytes 32 | tf_op jit(solution)/shard_map/psum | solution.py:84
  421.8 5.5 collective-permute-start.48
  428.6 2.0 collective-permute-start.44
  432.0 4.5 collective-permute-start.50
  437.9 2.1 collective-permute-start.46
  442.2 3.7 collective-permute-start.52
  445.9 1.6 collective-permute-start.53
  447.8 4.1 collective-permute-done.53
  452.4 2.1 gather_fusion.4
  454.6 18.5 %fusion.28 = f32[2]{0:T(128)S(1)} fusion(f32[2,1024]{1,0:T(2,128)S(1)} %get-tuple-element.203, f32[2,8,36,128]{3,0,2,1:T(2,128)S(1)} %bitcast.207, f32[8,36,128,128]{3,2,1,0:T(8,128)} %get-tuple-element.137, f32[1024]{0:T(1024)S(1)} %bitcast.211), kind=kOutput, calls=%fused_computation.61 | convolution fusion | flops 113254400 | bytes 19181576 | tf_op jit(solution)/shard_map/teij,ktej->kti/dot_general | solution.py:80
  473.1 44.1 %all-reduce.1 = (f32[2]{0:T(128)S(1)}, f32[2]{0:T(128)S(1)}) all-reduce(f32[2]{0:T(128)S(1)} %get-tuple-element.202, f32[2]{0:T(128)S(1)} %fusion.28), channel_id=1, replica_groups=mesh['gx'=4,'gy'=2,'gz'=4] {'gx','gy','gz'}, use_global_device_ids=true, to_apply=%region_16.17 | all-reduce | flops 4 | bytes 32 | tf_op jit(solution)/shard_map/psum | solution.py:84
  517.4 38.3 %psum.71 = f32[2]{0:T(128)S(1)} all-reduce(f32[2]{0:T(128)S(1)} %get-tuple-element.198), channel_id=1, replica_groups=mesh['gx'=4,'gy'=2,'gz'=4] {'gx','gy','gz'}, use_global_device_ids=true, to_apply=%region_20.21 | all-reduce | flops 2 | bytes 16 | tf_op jit(solution)/shard_map/psum | solution.py:132
  (287 shorter events, 75.4 us)
Async XLA Ops:
  0.6 0.7 copy-start
  2.7 38.9 %collective-permute-start.12 = (f32[1,1,1,5,1024]{4,3,2,1,0:T(8,128)S(1)}, f32[1,1,1,5,1024]{4,3,2,1,0:T(8,128)S(1)}, u32[]{:S(2)}, u32[]{:S(2)}) collective-permute-start(f32[1,1,1,5,1024]{4,3,2,1,0:T(8,128)S(1)} %maximum_bitcast_fusion), channel_id=1, source_target_pairs={{0,8},{8,16},{16,24},{1,9},{9,17},{17,25},{2,10},{10,18},{18,26},{... | collective-permute-start | bytes 61448 | tf_op jit(solution)/shard_map/ppermute | solution.py:22
  5.0 37.9 %collective-permute-start.13 = (f32[1,1,1,5,1024]{4,3,2,1,0:T(8,128)S(1)}, f32[1,1,1,5,1024]{4,3,2,1,0:T(8,128)S(1)}, u32[]{:S(2)}, u32[]{:S(2)}) collective-permute-start(f32[1,1,1,5,1024]{4,3,2,1,0:T(8,128)S(1)} %maximum_bitcast_fusion), channel_id=1, source_target_pairs={{8,0},{16,8},{24,16},{9,1},{17,9},{25,17},{10,2},{18,10},{26,18},{... | collective-permute-start | bytes 61448 | tf_op jit(solution)/shard_map/ppermute | solution.py:24
  7.5 12.7 %collective-permute-start = (f32[1,1,1,1,1024]{4,3,2,1,0:T(1,128)S(1)}, f32[1,1,1,1,1024]{4,3,2,1,0:T(1,128)S(1)}, u32[]{:S(2)}, u32[]{:S(2)}) collective-permute-start(f32[1,1,1,1,1024]{4,3,2,1,0:T(1,128)S(1)} %bitcast.212), channel_id=1, source_target_pairs={{0,8},{8,16},{16,24},{1,9},{9,17},{17,25},{2,10},{10,18},{18,26},{... | collective-permute-start | bytes 12296 | tf_op jit(solution)/shard_map/ppermute | solution.py:22
  12.6 8.8 %collective-permute-start.1 = (f32[1,1,1,1,1024]{4,3,2,1,0:T(1,128)S(1)}, f32[1,1,1,1,1024]{4,3,2,1,0:T(1,128)S(1)}, u32[]{:S(2)}, u32[]{:S(2)}) collective-permute-start(f32[1,1,1,1,1024]{4,3,2,1,0:T(1,128)S(1)} %bitcast.213), channel_id=1, source_target_pairs={{8,0},{16,8},{24,16},{9,1},{17,9},{25,17},{10,2},{18,10},{26,18},{... | collective-permute-start | bytes 12296 | tf_op jit(solution)/shard_map/ppermute | solution.py:24
  13.9 11.0 %collective-permute-start.6 = (f32[1,1,1,1,1024]{4,3,2,1,0:T(1,128)S(1)}, f32[1,1,1,1,1024]{4,3,2,1,0:T(1,128)S(1)}, u32[]{:S(2)}, u32[]{:S(2)}) collective-permute-start(f32[1,1,1,1,1024]{4,3,2,1,0:T(1,128)S(1)} %broadcast_in_dim_stack.7), channel_id=1, source_target_pairs={{0,8},{8,16},{16,24},{1,9},{9,17},{17,25},{2,10},{10,18},{18,26},{... | collective-permute-start | bytes 12296 | tf_op jit(solution)/shard_map/ppermute | solution.py:22
  20.2 6.0 %collective-permute-start.7 = (f32[1,1,1,1,1024]{4,3,2,1,0:T(1,128)S(1)}, f32[1,1,1,1,1024]{4,3,2,1,0:T(1,128)S(1)}, u32[]{:S(2)}, u32[]{:S(2)}) collective-permute-start(f32[1,1,1,1,1024]{4,3,2,1,0:T(1,128)S(1)} %broadcast_in_dim_stack.7), channel_id=1, source_target_pairs={{8,0},{16,8},{24,16},{9,1},{17,9},{25,17},{10,2},{18,10},{26,18},{... | collective-permute-start | bytes 12296 | tf_op jit(solution)/shard_map/ppermute | solution.py:24
  21.5 9.3 %collective-permute-start.2 = (f32[3,1,1,1,1024]{4,3,2,1,0:T(1,128)S(1)}, f32[3,1,1,1,1024]{4,3,2,1,0:T(1,128)S(1)}, u32[]{:S(2)}, u32[]{:S(2)}) collective-permute-start(f32[3,1,1,1,1024]{4,3,2,1,0:T(1,128)S(1)} %pad_maximum_fusion.11), channel_id=1, source_target_pairs={{0,4},{1,5},{2,6},{3,7},{8,12},{9,13},{10,14},{11,15},{16,20},{17,... | collective-permute-start | bytes 36872 | tf_op jit(solution)/shard_map/ppermute | solution.py:22
  24.9 7.2 %collective-permute-start.3 = (f32[3,1,1,1,1024]{4,3,2,1,0:T(1,128)S(1)}, f32[3,1,1,1,1024]{4,3,2,1,0:T(1,128)S(1)}, u32[]{:S(2)}, u32[]{:S(2)}) collective-permute-start(f32[3,1,1,1,1024]{4,3,2,1,0:T(1,128)S(1)} %pad_maximum_fusion.11), channel_id=1, source_target_pairs={{4,0},{5,1},{6,2},{7,3},{12,8},{13,9},{14,10},{15,11},{20,16},{21,... | collective-permute-start | bytes 36872 | tf_op jit(solution)/shard_map/ppermute | solution.py:24
  26.3 9.4 %collective-permute-start.8 = (f32[3,1,1,1,1024]{4,3,2,1,0:T(1,128)S(1)}, f32[3,1,1,1,1024]{4,3,2,1,0:T(1,128)S(1)}, u32[]{:S(2)}, u32[]{:S(2)}) collective-permute-start(f32[3,1,1,1,1024]{4,3,2,1,0:T(1,128)S(1)} %pad_maximum_fusion.12), channel_id=1, source_target_pairs={{0,4},{1,5},{2,6},{3,7},{8,12},{9,13},{10,14},{11,15},{16,20},{17,... | collective-permute-start | bytes 36872 | tf_op jit(solution)/shard_map/ppermute | solution.py:22
  30.8 6.2 %collective-permute-start.9 = (f32[3,1,1,1,1024]{4,3,2,1,0:T(1,128)S(1)}, f32[3,1,1,1,1024]{4,3,2,1,0:T(1,128)S(1)}, u32[]{:S(2)}, u32[]{:S(2)}) collective-permute-start(f32[3,1,1,1,1024]{4,3,2,1,0:T(1,128)S(1)} %pad_maximum_fusion.12), channel_id=1, source_target_pairs={{4,0},{5,1},{6,2},{7,3},{12,8},{13,9},{14,10},{15,11},{20,16},{21,... | collective-permute-start | bytes 36872 | tf_op jit(solution)/shard_map/ppermute | solution.py:24
  32.2 15.3 %collective-permute-start.4 = (f32[3,3,1,1,1024]{4,3,2,1,0:T(1,128)S(1)}, f32[3,3,1,1,1024]{4,3,2,1,0:T(1,128)S(1)}, u32[]{:S(2)}, u32[]{:S(2)}) collective-permute-start(f32[3,3,1,1,1024]{4,3,2,1,0:T(1,128)S(1)} %pad_maximum_fusion.3), channel_id=1, source_target_pairs={{0,1},{1,2},{2,3},{4,5},{5,6},{6,7},{8,9},{9,10},{10,11},{12,13},{... | collective-permute-start | bytes 110600 | tf_op jit(solution)/shard_map/ppermute | solution.py:22
  35.7 13.1 %collective-permute-start.5 = (f32[3,3,1,1,1024]{4,3,2,1,0:T(1,128)S(1)}, f32[3,3,1,1,1024]{4,3,2,1,0:T(1,128)S(1)}, u32[]{:S(2)}, u32[]{:S(2)}) collective-permute-start(f32[3,3,1,1,1024]{4,3,2,1,0:T(1,128)S(1)} %pad_maximum_fusion.3), channel_id=1, source_target_pairs={{1,0},{2,1},{3,2},{5,4},{6,5},{7,6},{9,8},{10,9},{11,10},{13,12},{... | collective-permute-start | bytes 110600 | tf_op jit(solution)/shard_map/ppermute | solution.py:24
  37.0 11.8 %collective-permute-start.10 = (f32[3,3,1,1,1024]{4,3,2,1,0:T(1,128)S(1)}, f32[3,3,1,1,1024]{4,3,2,1,0:T(1,128)S(1)}, u32[]{:S(2)}, u32[]{:S(2)}) collective-permute-start(f32[3,3,1,1,1024]{4,3,2,1,0:T(1,128)S(1)} %pad_maximum_fusion.4), channel_id=1, source_target_pairs={{0,1},{1,2},{2,3},{4,5},{5,6},{6,7},{8,9},{9,10},{10,11},{12,13},{... | collective-permute-start | bytes 110600 | tf_op jit(solution)/shard_map/ppermute | solution.py:22
  41.6 7.2 %collective-permute-start.11 = (f32[3,3,1,1,1024]{4,3,2,1,0:T(1,128)S(1)}, f32[3,3,1,1,1024]{4,3,2,1,0:T(1,128)S(1)}, u32[]{:S(2)}, u32[]{:S(2)}) collective-permute-start(f32[3,3,1,1,1024]{4,3,2,1,0:T(1,128)S(1)} %pad_maximum_fusion.4), channel_id=1, source_target_pairs={{1,0},{2,1},{3,2},{5,4},{6,5},{7,6},{9,8},{10,9},{11,10},{13,12},{... | collective-permute-start | bytes 110600 | tf_op jit(solution)/shard_map/ppermute | solution.py:24
  42.9 7.2 %collective-permute-start.14 = (f32[3,1,1,5,1024]{4,3,2,1,0:T(8,128)S(1)}, f32[3,1,1,5,1024]{4,3,2,1,0:T(8,128)S(1)}, u32[]{:S(2)}, u32[]{:S(2)}) collective-permute-start(f32[3,1,1,5,1024]{4,3,2,1,0:T(8,128)S(1)} %pad_maximum_fusion.2), channel_id=1, source_target_pairs={{0,4},{1,5},{2,6},{3,7},{8,12},{9,13},{10,14},{11,15},{16,20},{17,... | collective-permute-start | bytes 184328 | tf_op jit(solution)/shard_map/ppermute | solution.py:22
  47.5 6.7 %collective-permute-start.15 = (f32[3,1,1,5,1024]{4,3,2,1,0:T(8,128)S(1)}, f32[3,1,1,5,1024]{4,3,2,1,0:T(8,128)S(1)}, u32[]{:S(2)}, u32[]{:S(2)}) collective-permute-start(f32[3,1,1,5,1024]{4,3,2,1,0:T(8,128)S(1)} %pad_maximum_fusion.2), channel_id=1, source_target_pairs={{4,0},{5,1},{6,2},{7,3},{12,8},{13,9},{14,10},{15,11},{20,16},{21,... | collective-permute-start | bytes 184328 | tf_op jit(solution)/shard_map/ppermute | solution.py:24
  54.3 9.5 %collective-permute-start.16 = (f32[3,3,1,5,1024]{4,3,2,1,0:T(8,128)S(1)}, f32[3,3,1,5,1024]{4,3,2,1,0:T(8,128)S(1)}, u32[]{:S(2)}, u32[]{:S(2)}) collective-permute-start(f32[3,3,1,5,1024]{4,3,2,1,0:T(8,128)S(1)} %pad_maximum_fusion.1), channel_id=1, source_target_pairs={{0,1},{1,2},{2,3},{4,5},{5,6},{6,7},{8,9},{9,10},{10,11},{12,13},{... | collective-permute-start | bytes 552968 | tf_op jit(solution)/shard_map/ppermute | solution.py:22
  58.6 9.2 %collective-permute-start.17 = (f32[3,3,1,5,1024]{4,3,2,1,0:T(8,128)S(1)}, f32[3,3,1,5,1024]{4,3,2,1,0:T(8,128)S(1)}, u32[]{:S(2)}, u32[]{:S(2)}) collective-permute-start(f32[3,3,1,5,1024]{4,3,2,1,0:T(8,128)S(1)} %pad_maximum_fusion.1), channel_id=1, source_target_pairs={{1,0},{2,1},{3,2},{5,4},{6,5},{7,6},{9,8},{10,9},{11,10},{13,12},{... | collective-permute-start | bytes 552968 | tf_op jit(solution)/shard_map/ppermute | solution.py:24
  220.8 9.4 %collective-permute-start.18 = (f32[1,1,1,1,1024]{4,3,2,1,0:T(1,128)S(1)}, f32[1,1,1,1,1024]{4,3,2,1,0:T(1,128)S(1)}, u32[]{:S(2)}, u32[]{:S(2)}) collective-permute-start(f32[1,1,1,1,1024]{4,3,2,1,0:T(1,128)S(1)} %get-tuple-element.218), channel_id=1, source_target_pairs={{0,8},{8,16},{16,24},{1,9},{9,17},{17,25},{2,10},{10,18},{18,26},{... | collective-permute-start | bytes 12296 | tf_op jit(solution)/shard_map/ppermute | solution.py:22
  222.1 8.2 %collective-permute-start.19 = (f32[1,1,1,1,1024]{4,3,2,1,0:T(1,128)S(1)}, f32[1,1,1,1,1024]{4,3,2,1,0:T(1,128)S(1)}, u32[]{:S(2)}, u32[]{:S(2)}) collective-permute-start(f32[1,1,1,1,1024]{4,3,2,1,0:T(1,128)S(1)} %get-tuple-element.218), channel_id=1, source_target_pairs={{8,0},{16,8},{24,16},{9,1},{17,9},{25,17},{10,2},{18,10},{26,18},{... | collective-permute-start | bytes 12296 | tf_op jit(solution)/shard_map/ppermute | solution.py:24
  223.4 12.1 %collective-permute-start.24 = (f32[1,1,1,1,1024]{4,3,2,1,0:T(1,128)S(1)}, f32[1,1,1,1,1024]{4,3,2,1,0:T(1,128)S(1)}, u32[]{:S(2)}, u32[]{:S(2)}) collective-permute-start(f32[1,1,1,1,1024]{4,3,2,1,0:T(1,128)S(1)} %get-tuple-element.219), channel_id=1, source_target_pairs={{0,8},{8,16},{16,24},{1,9},{9,17},{17,25},{2,10},{10,18},{18,26},{... | collective-permute-start | bytes 12296 | tf_op jit(solution)/shard_map/ppermute | solution.py:22
  228.9 6.5 %collective-permute-start.25 = (f32[1,1,1,1,1024]{4,3,2,1,0:T(1,128)S(1)}, f32[1,1,1,1,1024]{4,3,2,1,0:T(1,128)S(1)}, u32[]{:S(2)}, u32[]{:S(2)}) collective-permute-start(f32[1,1,1,1,1024]{4,3,2,1,0:T(1,128)S(1)} %get-tuple-element.219), channel_id=1, source_target_pairs={{8,0},{16,8},{24,16},{9,1},{17,9},{25,17},{10,2},{18,10},{26,18},{... | collective-permute-start | bytes 12296 | tf_op jit(solution)/shard_map/ppermute | solution.py:24
  230.3 11.1 %collective-permute-start.20 = (f32[3,1,1,1,1024]{4,3,2,1,0:T(1,128)S(1)}, f32[3,1,1,1,1024]{4,3,2,1,0:T(1,128)S(1)}, u32[]{:S(2)}, u32[]{:S(2)}) collective-permute-start(f32[3,1,1,1,1024]{4,3,2,1,0:T(1,128)S(1)} %pad_maximum_fusion.13), channel_id=1, source_target_pairs={{0,4},{1,5},{2,6},{3,7},{8,12},{9,13},{10,14},{11,15},{16,20},{17,... | collective-permute-start | bytes 36872 | tf_op jit(solution)/shard_map/ppermute | solution.py:22
  234.2 7.2 %collective-permute-start.21 = (f32[3,1,1,1,1024]{4,3,2,1,0:T(1,128)S(1)}, f32[3,1,1,1,1024]{4,3,2,1,0:T(1,128)S(1)}, u32[]{:S(2)}, u32[]{:S(2)}) collective-permute-start(f32[3,1,1,1,1024]{4,3,2,1,0:T(1,128)S(1)} %pad_maximum_fusion.13), channel_id=1, source_target_pairs={{4,0},{5,1},{6,2},{7,3},{12,8},{13,9},{14,10},{15,11},{20,16},{21,... | collective-permute-start | bytes 36872 | tf_op jit(solution)/shard_map/ppermute | solution.py:24
  235.5 9.4 %collective-permute-start.26 = (f32[3,1,1,1,1024]{4,3,2,1,0:T(1,128)S(1)}, f32[3,1,1,1,1024]{4,3,2,1,0:T(1,128)S(1)}, u32[]{:S(2)}, u32[]{:S(2)}) collective-permute-start(f32[3,1,1,1,1024]{4,3,2,1,0:T(1,128)S(1)} %pad_maximum_fusion.14), channel_id=1, source_target_pairs={{0,4},{1,5},{2,6},{3,7},{8,12},{9,13},{10,14},{11,15},{16,20},{17,... | collective-permute-start | bytes 36872 | tf_op jit(solution)/shard_map/ppermute | solution.py:22
  240.1 5.6 %collective-permute-start.27 = (f32[3,1,1,1,1024]{4,3,2,1,0:T(1,128)S(1)}, f32[3,1,1,1,1024]{4,3,2,1,0:T(1,128)S(1)}, u32[]{:S(2)}, u32[]{:S(2)}) collective-permute-start(f32[3,1,1,1,1024]{4,3,2,1,0:T(1,128)S(1)} %pad_maximum_fusion.14), channel_id=1, source_target_pairs={{4,0},{5,1},{6,2},{7,3},{12,8},{13,9},{14,10},{15,11},{20,16},{21,... | collective-permute-start | bytes 36872 | tf_op jit(solution)/shard_map/ppermute | solution.py:24
  241.4 9.6 %collective-permute-start.22 = (f32[3,3,1,1,1024]{4,3,2,1,0:T(1,128)S(1)}, f32[3,3,1,1,1024]{4,3,2,1,0:T(1,128)S(1)}, u32[]{:S(2)}, u32[]{:S(2)}) collective-permute-start(f32[3,3,1,1,1024]{4,3,2,1,0:T(1,128)S(1)} %pad_maximum_fusion.5), channel_id=1, source_target_pairs={{0,1},{1,2},{2,3},{4,5},{5,6},{6,7},{8,9},{9,10},{10,11},{12,13},{... | collective-permute-start | bytes 110600 | tf_op jit(solution)/shard_map/ppermute | solution.py:22
  243.6 7.5 %collective-permute-start.23 = (f32[3,3,1,1,1024]{4,3,2,1,0:T(1,128)S(1)}, f32[3,3,1,1,1024]{4,3,2,1,0:T(1,128)S(1)}, u32[]{:S(2)}, u32[]{:S(2)}) collective-permute-start(f32[3,3,1,1,1024]{4,3,2,1,0:T(1,128)S(1)} %pad_maximum_fusion.5), channel_id=1, source_target_pairs={{1,0},{2,1},{3,2},{5,4},{6,5},{7,6},{9,8},{10,9},{11,10},{13,12},{... | collective-permute-start | bytes 110600 | tf_op jit(solution)/shard_map/ppermute | solution.py:24
  245.7 5.7 %collective-permute-start.28 = (f32[3,3,1,1,1024]{4,3,2,1,0:T(1,128)S(1)}, f32[3,3,1,1,1024]{4,3,2,1,0:T(1,128)S(1)}, u32[]{:S(2)}, u32[]{:S(2)}) collective-permute-start(f32[3,3,1,1,1024]{4,3,2,1,0:T(1,128)S(1)} %pad_maximum_fusion.6), channel_id=1, source_target_pairs={{0,1},{1,2},{2,3},{4,5},{5,6},{6,7},{8,9},{9,10},{10,11},{12,13},{... | collective-permute-start | bytes 110600 | tf_op jit(solution)/shard_map/ppermute | solution.py:22
  249.5 6.0 %collective-permute-start.29 = (f32[3,3,1,1,1024]{4,3,2,1,0:T(1,128)S(1)}, f32[3,3,1,1,1024]{4,3,2,1,0:T(1,128)S(1)}, u32[]{:S(2)}, u32[]{:S(2)}) collective-permute-start(f32[3,3,1,1,1024]{4,3,2,1,0:T(1,128)S(1)} %pad_maximum_fusion.6), channel_id=1, source_target_pairs={{1,0},{2,1},{3,2},{5,4},{6,5},{7,6},{9,8},{10,9},{11,10},{13,12},{... | collective-permute-start | bytes 110600 | tf_op jit(solution)/shard_map/ppermute | solution.py:24
  320.9 9.4 %collective-permute-start.30 = (f32[1,1,1,1,1024]{4,3,2,1,0:T(1,128)S(1)}, f32[1,1,1,1,1024]{4,3,2,1,0:T(1,128)S(1)}, u32[]{:S(2)}, u32[]{:S(2)}) collective-permute-start(f32[1,1,1,1,1024]{4,3,2,1,0:T(1,128)S(1)} %get-tuple-element.216), channel_id=1, source_target_pairs={{0,8},{8,16},{16,24},{1,9},{9,17},{17,25},{2,10},{10,18},{18,26},{... | collective-permute-start | bytes 12296 | tf_op jit(solution)/shard_map/ppermute | solution.py:22
  322.2 8.2 %collective-permute-start.31 = (f32[1,1,1,1,1024]{4,3,2,1,0:T(1,128)S(1)}, f32[1,1,1,1,1024]{4,3,2,1,0:T(1,128)S(1)}, u32[]{:S(2)}, u32[]{:S(2)}) collective-permute-start(f32[1,1,1,1,1024]{4,3,2,1,0:T(1,128)S(1)} %get-tuple-element.216), channel_id=1, source_target_pairs={{8,0},{16,8},{24,16},{9,1},{17,9},{25,17},{10,2},{18,10},{26,18},{... | collective-permute-start | bytes 12296 | tf_op jit(solution)/shard_map/ppermute | solution.py:24
  323.5 10.2 %collective-permute-start.36 = (f32[1,1,1,1,1024]{4,3,2,1,0:T(1,128)S(1)}, f32[1,1,1,1,1024]{4,3,2,1,0:T(1,128)S(1)}, u32[]{:S(2)}, u32[]{:S(2)}) collective-permute-start(f32[1,1,1,1,1024]{4,3,2,1,0:T(1,128)S(1)} %get-tuple-element.217), channel_id=1, source_target_pairs={{0,8},{8,16},{16,24},{1,9},{9,17},{17,25},{2,10},{10,18},{18,26},{... | collective-permute-start | bytes 12296 | tf_op jit(solution)/shard_map/ppermute | solution.py:22
  329.0 4.7 collective-permute-start.37
  330.3 9.2 %collective-permute-start.32 = (f32[3,1,1,1,1024]{4,3,2,1,0:T(1,128)S(1)}, f32[3,1,1,1,1024]{4,3,2,1,0:T(1,128)S(1)}, u32[]{:S(2)}, u32[]{:S(2)}) collective-permute-start(f32[3,1,1,1,1024]{4,3,2,1,0:T(1,128)S(1)} %pad_maximum_fusion.15), channel_id=1, source_target_pairs={{0,4},{1,5},{2,6},{3,7},{8,12},{9,13},{10,14},{11,15},{16,20},{17,... | collective-permute-start | bytes 36872 | tf_op jit(solution)/shard_map/ppermute | solution.py:22
  332.4 7.2 %collective-permute-start.33 = (f32[3,1,1,1,1024]{4,3,2,1,0:T(1,128)S(1)}, f32[3,1,1,1,1024]{4,3,2,1,0:T(1,128)S(1)}, u32[]{:S(2)}, u32[]{:S(2)}) collective-permute-start(f32[3,1,1,1,1024]{4,3,2,1,0:T(1,128)S(1)} %pad_maximum_fusion.15), channel_id=1, source_target_pairs={{4,0},{5,1},{6,2},{7,3},{12,8},{13,9},{14,10},{15,11},{20,16},{21,... | collective-permute-start | bytes 36872 | tf_op jit(solution)/shard_map/ppermute | solution.py:24
  333.7 9.3 %collective-permute-start.38 = (f32[3,1,1,1,1024]{4,3,2,1,0:T(1,128)S(1)}, f32[3,1,1,1,1024]{4,3,2,1,0:T(1,128)S(1)}, u32[]{:S(2)}, u32[]{:S(2)}) collective-permute-start(f32[3,1,1,1,1024]{4,3,2,1,0:T(1,128)S(1)} %pad_maximum_fusion.16), channel_id=1, source_target_pairs={{0,4},{1,5},{2,6},{3,7},{8,12},{9,13},{10,14},{11,15},{16,20},{17,... | collective-permute-start | bytes 36872 | tf_op jit(solution)/shard_map/ppermute | solution.py:22
  338.2 5.6 %collective-permute-start.39 = (f32[3,1,1,1,1024]{4,3,2,1,0:T(1,128)S(1)}, f32[3,1,1,1,1024]{4,3,2,1,0:T(1,128)S(1)}, u32[]{:S(2)}, u32[]{:S(2)}) collective-permute-start(f32[3,1,1,1,1024]{4,3,2,1,0:T(1,128)S(1)} %pad_maximum_fusion.16), channel_id=1, source_target_pairs={{4,0},{5,1},{6,2},{7,3},{12,8},{13,9},{14,10},{15,11},{20,16},{21,... | collective-permute-start | bytes 36872 | tf_op jit(solution)/shard_map/ppermute | solution.py:24
  339.6 9.6 %collective-permute-start.34 = (f32[3,3,1,1,1024]{4,3,2,1,0:T(1,128)S(1)}, f32[3,3,1,1,1024]{4,3,2,1,0:T(1,128)S(1)}, u32[]{:S(2)}, u32[]{:S(2)}) collective-permute-start(f32[3,3,1,1,1024]{4,3,2,1,0:T(1,128)S(1)} %pad_maximum_fusion.7), channel_id=1, source_target_pairs={{0,1},{1,2},{2,3},{4,5},{5,6},{6,7},{8,9},{9,10},{10,11},{12,13},{... | collective-permute-start | bytes 110600 | tf_op jit(solution)/shard_map/ppermute | solution.py:22
  341.7 7.5 %collective-permute-start.35 = (f32[3,3,1,1,1024]{4,3,2,1,0:T(1,128)S(1)}, f32[3,3,1,1,1024]{4,3,2,1,0:T(1,128)S(1)}, u32[]{:S(2)}, u32[]{:S(2)}) collective-permute-start(f32[3,3,1,1,1024]{4,3,2,1,0:T(1,128)S(1)} %pad_maximum_fusion.7), channel_id=1, source_target_pairs={{1,0},{2,1},{3,2},{5,4},{6,5},{7,6},{9,8},{10,9},{11,10},{13,12},{... | collective-permute-start | bytes 110600 | tf_op jit(solution)/shard_map/ppermute | solution.py:24
  343.9 5.6 %collective-permute-start.40 = (f32[3,3,1,1,1024]{4,3,2,1,0:T(1,128)S(1)}, f32[3,3,1,1,1024]{4,3,2,1,0:T(1,128)S(1)}, u32[]{:S(2)}, u32[]{:S(2)}) collective-permute-start(f32[3,3,1,1,1024]{4,3,2,1,0:T(1,128)S(1)} %pad_maximum_fusion.8), channel_id=1, source_target_pairs={{0,1},{1,2},{2,3},{4,5},{5,6},{6,7},{8,9},{9,10},{10,11},{12,13},{... | collective-permute-start | bytes 110600 | tf_op jit(solution)/shard_map/ppermute | solution.py:22
  347.7 6.0 %collective-permute-start.41 = (f32[3,3,1,1,1024]{4,3,2,1,0:T(1,128)S(1)}, f32[3,3,1,1,1024]{4,3,2,1,0:T(1,128)S(1)}, u32[]{:S(2)}, u32[]{:S(2)}) collective-permute-start(f32[3,3,1,1,1024]{4,3,2,1,0:T(1,128)S(1)} %pad_maximum_fusion.8), channel_id=1, source_target_pairs={{1,0},{2,1},{3,2},{5,4},{6,5},{7,6},{9,8},{10,9},{11,10},{13,12},{... | collective-permute-start | bytes 110600 | tf_op jit(solution)/shard_map/ppermute | solution.py:24
  419.2 9.4 %collective-permute-start.42 = (f32[1,1,1,1,1024]{4,3,2,1,0:T(1,128)S(1)}, f32[1,1,1,1,1024]{4,3,2,1,0:T(1,128)S(1)}, u32[]{:S(2)}, u32[]{:S(2)}) collective-permute-start(f32[1,1,1,1,1024]{4,3,2,1,0:T(1,128)S(1)} %get-tuple-element.214), channel_id=1, source_target_pairs={{0,8},{8,16},{16,24},{1,9},{9,17},{17,25},{2,10},{10,18},{18,26},{... | collective-permute-start | bytes 12296 | tf_op jit(solution)/shard_map/ppermute | solution.py:22
  420.5 8.2 %collective-permute-start.43 = (f32[1,1,1,1,1024]{4,3,2,1,0:T(1,128)S(1)}, f32[1,1,1,1,1024]{4,3,2,1,0:T(1,128)S(1)}, u32[]{:S(2)}, u32[]{:S(2)}) collective-permute-start(f32[1,1,1,1,1024]{4,3,2,1,0:T(1,128)S(1)} %get-tuple-element.214), channel_id=1, source_target_pairs={{8,0},{16,8},{24,16},{9,1},{17,9},{25,17},{10,2},{18,10},{26,18},{... | collective-permute-start | bytes 12296 | tf_op jit(solution)/shard_map/ppermute | solution.py:24
  421.8 10.2 %collective-permute-start.48 = (f32[1,1,1,1,1024]{4,3,2,1,0:T(1,128)S(1)}, f32[1,1,1,1,1024]{4,3,2,1,0:T(1,128)S(1)}, u32[]{:S(2)}, u32[]{:S(2)}) collective-permute-start(f32[1,1,1,1,1024]{4,3,2,1,0:T(1,128)S(1)} %get-tuple-element.215), channel_id=1, source_target_pairs={{0,8},{8,16},{16,24},{1,9},{9,17},{17,25},{2,10},{10,18},{18,26},{... | collective-permute-start | bytes 12296 | tf_op jit(solution)/shard_map/ppermute | solution.py:22
  427.3 4.7 collective-permute-start.49
  428.6 9.2 %collective-permute-start.44 = (f32[3,1,1,1,1024]{4,3,2,1,0:T(1,128)S(1)}, f32[3,1,1,1,1024]{4,3,2,1,0:T(1,128)S(1)}, u32[]{:S(2)}, u32[]{:S(2)}) collective-permute-start(f32[3,1,1,1,1024]{4,3,2,1,0:T(1,128)S(1)} %pad_maximum_fusion.17), channel_id=1, source_target_pairs={{0,4},{1,5},{2,6},{3,7},{8,12},{9,13},{10,14},{11,15},{16,20},{17,... | collective-permute-start | bytes 36872 | tf_op jit(solution)/shard_map/ppermute | solution.py:22
  430.7 7.2 %collective-permute-start.45 = (f32[3,1,1,1,1024]{4,3,2,1,0:T(1,128)S(1)}, f32[3,1,1,1,1024]{4,3,2,1,0:T(1,128)S(1)}, u32[]{:S(2)}, u32[]{:S(2)}) collective-permute-start(f32[3,1,1,1,1024]{4,3,2,1,0:T(1,128)S(1)} %pad_maximum_fusion.17), channel_id=1, source_target_pairs={{4,0},{5,1},{6,2},{7,3},{12,8},{13,9},{14,10},{15,11},{20,16},{21,... | collective-permute-start | bytes 36872 | tf_op jit(solution)/shard_map/ppermute | solution.py:24
  432.0 9.3 %collective-permute-start.50 = (f32[3,1,1,1,1024]{4,3,2,1,0:T(1,128)S(1)}, f32[3,1,1,1,1024]{4,3,2,1,0:T(1,128)S(1)}, u32[]{:S(2)}, u32[]{:S(2)}) collective-permute-start(f32[3,1,1,1,1024]{4,3,2,1,0:T(1,128)S(1)} %pad_maximum_fusion.18), channel_id=1, source_target_pairs={{0,4},{1,5},{2,6},{3,7},{8,12},{9,13},{10,14},{11,15},{16,20},{17,... | collective-permute-start | bytes 36872 | tf_op jit(solution)/shard_map/ppermute | solution.py:22
  436.6 5.6 %collective-permute-start.51 = (f32[3,1,1,1,1024]{4,3,2,1,0:T(1,128)S(1)}, f32[3,1,1,1,1024]{4,3,2,1,0:T(1,128)S(1)}, u32[]{:S(2)}, u32[]{:S(2)}) collective-permute-start(f32[3,1,1,1,1024]{4,3,2,1,0:T(1,128)S(1)} %pad_maximum_fusion.18), channel_id=1, source_target_pairs={{4,0},{5,1},{6,2},{7,3},{12,8},{13,9},{14,10},{15,11},{20,16},{21,... | collective-permute-start | bytes 36872 | tf_op jit(solution)/shard_map/ppermute | solution.py:24
  437.9 9.6 %collective-permute-start.46 = (f32[3,3,1,1,1024]{4,3,2,1,0:T(1,128)S(1)}, f32[3,3,1,1,1024]{4,3,2,1,0:T(1,128)S(1)}, u32[]{:S(2)}, u32[]{:S(2)}) collective-permute-start(f32[3,3,1,1,1024]{4,3,2,1,0:T(1,128)S(1)} %pad_maximum_fusion.9), channel_id=1, source_target_pairs={{0,1},{1,2},{2,3},{4,5},{5,6},{6,7},{8,9},{9,10},{10,11},{12,13},{... | collective-permute-start | bytes 110600 | tf_op jit(solution)/shard_map/ppermute | solution.py:22
  440.0 7.5 %collective-permute-start.47 = (f32[3,3,1,1,1024]{4,3,2,1,0:T(1,128)S(1)}, f32[3,3,1,1,1024]{4,3,2,1,0:T(1,128)S(1)}, u32[]{:S(2)}, u32[]{:S(2)}) collective-permute-start(f32[3,3,1,1,1024]{4,3,2,1,0:T(1,128)S(1)} %pad_maximum_fusion.9), channel_id=1, source_target_pairs={{1,0},{2,1},{3,2},{5,4},{6,5},{7,6},{9,8},{10,9},{11,10},{13,12},{... | collective-permute-start | bytes 110600 | tf_op jit(solution)/shard_map/ppermute | solution.py:24
  442.2 5.6 %collective-permute-start.52 = (f32[3,3,1,1,1024]{4,3,2,1,0:T(1,128)S(1)}, f32[3,3,1,1,1024]{4,3,2,1,0:T(1,128)S(1)}, u32[]{:S(2)}, u32[]{:S(2)}) collective-permute-start(f32[3,3,1,1,1024]{4,3,2,1,0:T(1,128)S(1)} %pad_maximum_fusion.10), channel_id=1, source_target_pairs={{0,1},{1,2},{2,3},{4,5},{5,6},{6,7},{8,9},{9,10},{10,11},{12,13},{... | collective-permute-start | bytes 110600 | tf_op jit(solution)/shard_map/ppermute | solution.py:22
  445.9 6.0 %collective-permute-start.53 = (f32[3,3,1,1,1024]{4,3,2,1,0:T(1,128)S(1)}, f32[3,3,1,1,1024]{4,3,2,1,0:T(1,128)S(1)}, u32[]{:S(2)}, u32[]{:S(2)}) collective-permute-start(f32[3,3,1,1,1024]{4,3,2,1,0:T(1,128)S(1)} %pad_maximum_fusion.10), channel_id=1, source_target_pairs={{1,0},{2,1},{3,2},{5,4},{6,5},{7,6},{9,8},{10,9},{11,10},{13,12},{... | collective-permute-start | bytes 110600 | tf_op jit(solution)/shard_map/ppermute | solution.py:24
  517.4 40.9 %copy-start.1 = (f32[2,1024]{1,0:T(2,128)}, f32[2,1024]{1,0:T(2,128)S(1)}, u32[]{:S(2)}) copy-start(f32[2,1024]{1,0:T(2,128)S(1)} %get-tuple-element.199) | copy-start | bytes 24580
where the time goes:
time: 561 us; the launch traced here: 558 us
  blocking collectives  211 us (38%)
  starting transfers between devices  132 us (24%)
  other arithmetic  79.6 us (14%)
  matrix products  77.7 us (14%)
  waiting for transfers between devices  26.1 us (5%)
  local copies, waits for them, and re-layouts  22.4 us (4%)
  loops' own time  5.87 us (1%)
    psum x4, blocking collectives, two_products(): lax.psum((jnp.sum(residual * residual, axis=1), jnp.sum(residual * image,...  173 us
    ppermute x27, starting transfers between devices, padded(): lax.ppermute(tail, axis, [(i, (i + 1) % count) for i in range(ends)])  96.3 us
    dot_general x4, matrix products, couple(): jnp.einsum('teij,ktej->kti', blocks, picked, precision=lax.Precision.HIGH...  74.3 us
    dynamic_update_slice x8, other arithmetic, tile_blocks(): lax.map(one_tile, (mine_all, tile_lists, jnp.arange(tile_count, dtype=jnp...  48.9 us
    psum x1, blocking collectives, on_device(): sums = lax.psum(jnp.sum(solution, axis=1), ('gx', 'gy', 'gz'))  38.3 us
    ppermute x27, starting transfers between devices, padded(): lax.ppermute(head, axis, [((i + 1) % count, i) for i in range(ends)])  35.8 us
    ppermute x27, waiting for transfers between devices, padded(): lax.ppermute(head, axis, [((i + 1) % count, i) for i in range(ends)])  23 us
  transfers between devices with their start and end apart: 54, of which 13 were waited for; matrix products, arithmetic and copies ran while one was open for 1% of the time, Pallas kernels for 0%

commit v1 on v0

v1 whole, which is shorter than its diff:
```python
import functools
import math

import jax
import jax.numpy as jnp
from jax import lax
from jax.experimental import pallas as pl
from jax.experimental.pallas import tpu as pltpu
from jax.sharding import PartitionSpec as P

ITERS = 4
CUTOFF = 10.0
COULOMB = 0.3
VOLUME = 10.0
MESH = pl.DeviceIdType.MESH
AXES = ("gx", "gy", "gz")
FAR = 100.0
DEPTH = 48


def total(a):
    return jnp.sum(jnp.sum(a, axis=0, keepdims=True), axis=1, keepdims=True)


def split(a):
    first = a.astype(jnp.bfloat16)
    rest = a - first.astype(jnp.float32)
    second = rest.astype(jnp.bfloat16)
    third = (rest - second.astype(jnp.float32)).astype(jnp.bfloat16)
    return [p.astype(jnp.float32) for p in (first, second, third)]


def kernel(
    grid, unroll, lists, hardness, electroneg, gamma, geo,
    charges, solution_ref,
    geo_halo, vec_halos, shares, features, lhs, weights, weight_col,
    current0, current1, eta_rows, gamma_rows, diagonal, image0, image1, blocks,
    geo_send, geo_recv, vec_sends, vec_recvs, sum_sends, sum_recvs,
):
    tiles, nbr = lists.shape
    kinds = gamma.shape[0]
    width = geo.shape[2]
    devices = math.prod(grid)
    scale = (tiles * width * VOLUME) ** (1.0 / 3.0) / CUTOFF
    me = [lax.axis_index(a) for a in AXES]
    my_id = (me[0] * grid[1] + me[1]) * grid[2] + me[2]

    def device_of(d):
        return (d // (grid[1] * grid[2]), (d // grid[2]) % grid[1], d % grid[2])

    def neighbour(o):
        where = (me[0] + o // 9 - 1, me[1] + (o // 3) % 3 - 1, me[2] + o % 3 - 1)
        there = functools.reduce(
            jnp.logical_and,
            [jnp.logical_and(w >= 0, w < g) for w, g in zip(where, grid)],
        )
        return where, there

    barrier = pltpu.get_barrier_semaphore()

    @pl.loop(1, devices)
    def _(j):
        d = lax.rem(my_id + j, devices)
        pl.semaphore_signal(barrier, inc=1, device_id=device_of(d), device_id_type=MESH)

    pl.semaphore_wait(barrier, devices - 1)

    def halo_copy(buffer, send, recv, slot, o, where):
        return pltpu.make_async_remote_copy(
            src_ref=buffer.at[13],
            dst_ref=buffer.at[slot],
            send_sem=send.at[o],
            recv_sem=recv.at[slot],
            device_id=where,
            device_id_type=MESH,
        )

    def each_neighbour(do):
        @pl.loop(0, 27)
        def _(o):
            where, there = neighbour(o)

            @pl.when(jnp.logical_and(there, o != 13))
            def _():
                do(o, where)

    def start_halo(buffer, send, recv):
        each_neighbour(lambda o, w: halo_copy(buffer, send, recv, 26 - o, o, w).start())

    def end_send(buffer, send, recv):
        each_neighbour(lambda o, w: halo_copy(buffer, send, recv, 26 - o, o, w).wait_send())

    def sum_copy(k, slot, j):
        return pltpu.make_async_remote_copy(
            src_ref=shares[k].at[0],
            dst_ref=shares[k].at[slot],
            send_sem=sum_sends[k].at[j],
            recv_sem=sum_recvs[k].at[slot],
            device_id=device_of(lax.rem(my_id + j, devices)),
            device_id_type=MESH,
        )

    def each_other(do):
        @pl.loop(1, devices)
        def _(j):
            do(j)

    geo_halo[13] = geo[...]
    start_halo(geo_halo, geo_send, geo_recv)

    row = lax.broadcasted_iota(jnp.int32, (8, width), 0)
    lane = lax.broadcasted_iota(jnp.int32, (1, width), 1)

    def look_up(table, kind):
        value = jnp.full(kind.shape, table[0], jnp.float32)
        for k in range(1, kinds):
            value = jnp.where(kind == float(k), table[k], value)
        return value

    def prepare(o, mine):
        where, there = neighbour(o)
        shift = [(o // 9 - 1), (o // 3) % 3 - 1, o % 3 - 1]
        shift = [s.astype(jnp.float32) - 0.5 if not mine else jnp.float32(-0.5) for s in shift]
        shifts = jnp.where(row == 0, shift[0], jnp.where(row == 1, shift[1], shift[2]))
        for pair in range(tiles // 2):
            data = jnp.where(there, geo_halo[o, pair], 0.0)
            gammas = look_up(gamma, data)
            w8 = jnp.exp2(jnp.log(gammas) * (-1.5 / math.log(2.0))) * CUTOFF**-1.5
            chi8 = jnp.where(there, -look_up(electroneg, data), 0.0)
            if mine:
                eta8 = look_up(hardness, data)
            for half in range(2):
                u = pair * 2 + half
                entry = o * tiles + u
                r3 = half * 4 + 3
                raw = data if half == 0 else pltpu.roll(data, 4, 0)
                at = (raw + shifts) * scale
                norm = jnp.sum(jnp.where(row < 3, at * at, 0.0), axis=0, keepdims=True)
                norm = jnp.where(there, norm, FAR)
                at = jnp.where(there, at, 0.0)
                b = jnp.where(row < 3, -2.0 * at, jnp.where(row == 3, 1.0, jnp.where(row == 4, norm, 0.0)))
                b1, b2, b3 = split(b)
                features[entry] = jnp.concatenate([b1, b2, b1, b2, b3, b1], axis=0).astype(jnp.bfloat16)
                weights[pl.ds(entry, 1), :] = w8[r3 : r3 + 1]
                current0[pl.ds(entry, 1), :] = chi8[r3 : r3 + 1]
                current1[pl.ds(entry, 1), :] = jnp.where(there, jnp.full((1, width), -1.0, jnp.float32), 0.0)
                if mine:
                    a = jnp.where(row < 3, at, jnp.where(row == 3, norm, jnp.where(row == 4, 1.0, 0.0)))
                    a1, a2, a3 = split(a)
                    rows = jnp.concatenate(
                        [a1, a1, a2, a2, a1, a3, jnp.zeros((width - DEPTH, width), jnp.float32)], axis=0
                    )
                    lhs[u] = jnp.transpose(rows).astype(jnp.bfloat16)
                    weight_col[u] = jnp.transpose(jnp.broadcast_to(w8[r3 : r3 + 1], (width, width)))
                    eta_rows[pl.ds(u, 1), :] = eta8[r3 : r3 + 1]
                    gamma_rows[pl.ds(u, 1), :] = gammas[r3 : r3 + 1]

    prepare(13, True)

    @pl.loop(0, 27)
    def _(o):
        where, there = neighbour(o)

        @pl.when(jnp.logical_and(there, o != 13))
        def _():
            halo_copy(geo_halo, geo_send, geo_recv, o, o, where).wait_recv()

        @pl.when(o != 13)
        def _():
            prepare(o, False)

    lanes_zero = jnp.zeros((width, width), jnp.float32)

    def row_sum(acc):
        return jnp.sum(jnp.transpose(acc), axis=0, keepdims=True)

    @pl.loop(0, tiles)
    def _(t):
        mine = lhs[t][:, :DEPTH]

        def step(g, carry):
            acc0, acc1, selves = carry
            for i in range(unroll):
                e = g * unroll + i
                entry = lists[t, e]
                x2 = jnp.dot(mine, features[entry], preferred_element_type=jnp.float32)
                x2 = jnp.maximum(x2, 1e-10)
                x = x2 * lax.rsqrt(x2)
                c = x2 * x + weight_col[t] * weights[pl.ds(entry, 1), :]
                inverse = jnp.exp2(jnp.log(c) * (-1.0 / (3.0 * math.log(2.0))))
                near = jnp.maximum(1.0 - x, 0.0)
                near = near * near
                f = COULOMB / CUTOFF
                taper = ((20.0 * f * x + 10.0 * f) * x + 4.0 * f) * x + f
                h = (near * near) * (taper * inverse)
                blocks[t * nbr + e] = h
                acc0 = acc0 + h * current0[pl.ds(entry, 1), :]
                acc1 = acc1 - h
                selves = selves + jnp.where(entry == 13 * tiles + t, 1, 0)
            return acc0, acc1, selves

        acc0, acc1, selves = lax.fori_loop(
            0, nbr // unroll, step, (lanes_zero, lanes_zero, jnp.int32(0))
        )
        image0[pl.ds(t, 1), :] = row_sum(acc0)
        image1[pl.ds(t, 1), :] = row_sum(acc1)
        diagonal[pl.ds(t, 1), :] = (
            eta_rows[pl.ds(t, 1), :]
            - selves.astype(jnp.float32) * COULOMB * gamma_rows[pl.ds(t, 1), :]
        )

    def couple():
        @pl.loop(0, tiles)
        def _(t):
            def step(g, carry):
                acc0, acc1 = carry
                for i in range(unroll):
                    e = g * unroll + i
                    entry = lists[t, e]
                    h = blocks[t * nbr + e]
                    acc0 = acc0 + h * current0[pl.ds(entry, 1), :]
                    acc1 = acc1 + h * current1[pl.ds(entry, 1), :]
                return acc0, acc1

            acc0, acc1 = lax.fori_loop(0, nbr // unroll, step, (lanes_zero, lanes_zero))
            image0[pl.ds(t, 1), :] = row_sum(acc0)
            image1[pl.ds(t, 1), :] = row_sum(acc1)

    systems = range(2)
    images = (image0, image1)
    currents = (current0, current1)
    diag = diagonal[...]
    r = [c[pl.ds(13 * tiles, tiles), :] for c in currents]
    w = [diag * r[s] + images[s][...] for s in systems]
    p = along = deep = None
    x = [jnp.zeros_like(r[0]) for s in systems]
    sum_x = [jnp.zeros((1, 1), jnp.float32) for s in systems]
    sum_p = rr_old = alpha = None
    for k in range(ITERS):
        parts = [
            jnp.where(
                lane == 0, total(r[s] * r[s]),
                jnp.where(lane == 1, total(r[s] * w[s]), jnp.where(lane == 2, total(r[s]), 0.0)),
            )
            for s in systems
        ]
        shares[k][0] = jnp.concatenate(parts, axis=0)
        last = k + 1 == ITERS
        if not last:
            buffer, send, recv = vec_halos[k], vec_sends[k], vec_recvs[k]
            for s in systems:
                buffer[13, s] = w[s]
            start_halo(buffer, send, recv)
        each_other(lambda j: sum_copy(k, devices - j, j).start())
        if not last:
            @pl.loop(0, 27)
            def _(o):
                where, there = neighbour(o)

                @pl.when(jnp.logical_and(there, o != 13))
                def _():
                    halo_copy(buffer, send, recv, o, o, where).wait_recv()

                start = pl.multiple_of(o * tiles, tiles)
                for s in systems:
                    currents[s][pl.ds(start, tiles), :] = jnp.where(there, buffer[o, s], 0.0)

            couple()
            q = [diag * w[s] + images[s][...] for s in systems]
        each_other(lambda j: sum_copy(k, j, j).wait_recv())
        sums = jnp.sum(shares[k][...], axis=0)
        rr, rw, sr = [
            [jnp.sum(jnp.where(lane == i, sums[s : s + 1], 0.0), axis=1, keepdims=True) for s in systems]
            for i in range(3)
        ]
        if k == 0:
            alpha = [rr[s] / rw[s] for s in systems]
            p, along, sum_p = list(r), list(w), sr
            if not last:
                deep = q
        else:
            beta = [rr[s] / rr_old[s] for s in systems]
            alpha = [rr[s] / (rw[s] - beta[s] * rr[s] / alpha[s]) for s in systems]
            p = [r[s] + beta[s] * p[s] for s in systems]
            sum_p = [sr[s] + beta[s] * sum_p[s] for s in systems]
            if not last:
                along = [w[s] + beta[s] * along[s] for s in systems]
                deep = [q[s] + beta[s] * deep[s] for s in systems]
        x = [x[s] + alpha[s] * p[s] for s in systems]
        sum_x = [sum_x[s] + alpha[s] * sum_p[s] for s in systems]
        rr_old = rr
        if not last:
            r = [r[s] - alpha[s] * along[s] for s in systems]
            w = [w[s] - alpha[s] * deep[s] for s in systems]

    for s in systems:
        solution_ref[s] = x[s]
    charges[...] = x[0] - (sum_x[0] / sum_x[1]) * x[1]

    end_send(geo_halo, geo_send, geo_recv)
    for k in range(ITERS - 1):
        end_send(vec_halos[k], vec_sends[k], vec_recvs[k])
    for k in range(ITERS):
        each_other(lambda j: sum_copy(k, devices - j, j).wait_send())


def on_device(positions, types, tile_lists, hardness, electroneg, gamma_table):
    atoms = positions.shape[4]
    tiles, nbr = tile_lists.shape
    width = atoms // tiles
    grid = tuple(lax.axis_size(a) for a in AXES)
    devices = math.prod(grid)
    unroll = next(u for u in (4, 3, 2, 1) if nbr % u == 0)
    geo = jnp.concatenate(
        [
            jnp.transpose(positions.reshape(3, tiles, width), (1, 0, 2)),
            types.reshape(tiles, 1, width).astype(jnp.float32),
        ],
        axis=1,
    ).reshape(tiles // 2, 8, width)
    f32 = jnp.float32
    vmem = pl.BlockSpec(memory_space=pltpu.VMEM)
    smem = pl.BlockSpec(memory_space=pltpu.SMEM)
    rounds = ITERS - 1
    charges, solution_ = pl.pallas_call(
        functools.partial(kernel, grid, unroll),
        out_shape=(
            jax.ShapeDtypeStruct((tiles, width), f32),
            jax.ShapeDtypeStruct((2, tiles, width), f32),
        ),
        in_specs=[smem] * 4 + [vmem],
        out_specs=(vmem, vmem),
        scratch_shapes=[
            pltpu.VMEM((27, tiles // 2, 8, width), f32),
            [pltpu.VMEM((27, 2, tiles, width), f32)] * rounds,
            [pltpu.VMEM((devices, 2, width), f32)] * ITERS,
            pltpu.VMEM((27 * tiles, DEPTH, width), jnp.bfloat16),
            pltpu.VMEM((tiles, width, width), jnp.bfloat16),
            pltpu.VMEM((27 * tiles, width), f32),
            pltpu.VMEM((tiles, width, width), f32),
            pltpu.VMEM((27 * tiles, width), f32),
            pltpu.VMEM((27 * tiles, width), f32),
            pltpu.VMEM((tiles, width), f32),
            pltpu.VMEM((tiles, width), f32),
            pltpu.VMEM((tiles, width), f32),
            pltpu.VMEM((tiles, width), f32),
            pltpu.VMEM((tiles, width), f32),
            pltpu.VMEM((tiles * nbr, width, width), f32),
            pltpu.SemaphoreType.DMA((27,)),
            pltpu.SemaphoreType.DMA((27,)),
            [pltpu.SemaphoreType.DMA((27,))] * rounds,
            [pltpu.SemaphoreType.DMA((27,))] * rounds,
            [pltpu.SemaphoreType.DMA((devices,))] * ITERS,
            [pltpu.SemaphoreType.DMA((devices,))] * ITERS,
        ],
        compiler_params=pltpu.CompilerParams(
            collective_id=0, has_side_effects=True, vmem_limit_bytes=56 * 2**20
        ),
    )(tile_lists, hardness, electroneg, gamma_table, geo)
    return charges.reshape(1, 1, 1, atoms), solution_.reshape(1, 1, 1, 2, atoms)


def solution(mesh):
    in_specs = (P("gx", "gy", "gz", None, None), P("gx", "gy", "gz", None), P(), P(), P(), P())
    out_specs = (P("gx", "gy", "gz", None), P("gx", "gy", "gz", None, None))
    return jax.shard_map(
        on_device, mesh=mesh, in_specs=in_specs, out_specs=out_specs, check_vma=False
    )
```

time: 561 us -> 86.8 us (0.15)
  blocking collectives: 211 us -> 0 us
  starting transfers between devices: 132 us -> 0 us
  Pallas kernels: 0 us -> 81.9 us
  other arithmetic: 79.6 us -> 1.3 us
  matrix products: 77.7 us -> 0 us
  waiting for transfers between devices: 26.1 us -> 0 us
  local copies, waits for them, and re-layouts: 22.4 us -> 2.61 us
  loops' own time: 5.87 us -> 0 us
    psum x5 -> x0, blocking collectives: 211 us -> none  [the longest x4 173 us: two_products(): lax.psum((jnp.sum(residual * residual, axis=1), jnp.sum(residual * image,...]
    ppermute x54 -> x0, starting transfers between devices: 132 us -> none  [the longest x27 96.3 us: padded(): lax.ppermute(tail, axis, [(i, (i + 1) % count) for i in range(ends)])]
    pallas_call x0 -> x1, Pallas kernels: none -> 81.9 us  [on_device(): pl.pallas_call(functools.partial(kernel, grid, unroll), out_shape=(jax.Sh...]
    dot_general x7 -> x0, matrix products: 77.7 us -> none  [the longest x4 74.3 us: couple(): jnp.einsum('teij,ktej->kti', blocks, picked, precision=lax.Precision.HIGH...]
    dynamic_update_slice x8 -> x0, other arithmetic: 48.9 us -> none  [tile_blocks(): lax.map(one_tile, (mine_all, tile_lists, jnp.arange(tile_count, dtype=jnp...]
    ppermute x54 -> x0, waiting for transfers between devices: 26.1 us -> none  [the longest x27 23 us: padded(): lax.ppermute(head, axis, [((i + 1) % count, i) for i in range(ends)])]
    gather x12 -> x0, local copies, waits for them, and re-layouts: 13.3 us -> none  [the longest x4 8.54 us: couple(): picked = nearby_vectors[:, tile_lists]]
    reduce_sum x10 -> x0, other arithmetic: 9.54 us -> none  [the longest x8 9.13 us: one_tile(): spacing = jnp.sqrt(jnp.sum(separation * separation, axis=0))]
  transfers between devices with their start and end apart: 54 -> 0, of which waited for: 13 -> 0; matrix products, arithmetic and copies ran while one was open for 1% -> 0% of each run, Pallas kernels for 0% -> 0%
where the time goes in v1:
time: 86.8 us; the launch traced here: 86.4 us
  Pallas kernels  81.9 us (94%)
  local copies, waits for them, and re-layouts  2.61 us (3%)
  other arithmetic  1.3 us (1%)
    pallas_call x1, Pallas kernels, on_device(): pl.pallas_call(functools.partial(kernel, grid, unroll), out_shape=(jax.Sh...  81.9 us

profile of v1, /device:TPU:0, one launch (start us, length us, event | category | flops | bytes accessed | tf_op | source)
XLA Modules:
  0.0 86.4 jit_solution(119995625565089206)
XLA Ops:
  0.6 0.7 convert_bitcast_fusion
  1.3 0.7 copy.11
  2.0 0.6 pad_maximum_fusion
  2.6 81.9 %shard_map.77 = (f32[8,128]{1,0:T(8,128)}, f32[2,8,128]{2,1,0:T(8,128)}) custom-call(s32[8,36]{1,0:T(8,128)} %lists.1, f32[4]{0:T(128)} %hardness.1, f32[4]{0:T(128)} %electroneg.1, f32[4]{0:T(128)} %gamma.1, f32[4,8,128]{2,1,0:T(8,128)} %bitcast.11), custom_call_target="tpu_custom_call" | custom-call | tf_op jit(solution)/shard_map/pallas_call | solution.py:325
  84.5 0.0 copy-start
  84.5 1.3 %reshape.33 = f32[1,1,1,2,1024]{4,3,2,1,0:T(2,128)} reshape(f32[2,8,128]{2,1,0:T(8,128)} %get-tuple-element.5) | data formatting | bytes 16384 | tf_op jit(solution)/shard_map/reshape | solution.py:360
  85.8 0.0 copy-done
  85.8 0.6 copy.13
Async XLA Ops:
  84.5 1.3 %copy-start = (f32[8,128]{1,0:T(8,128)S(1)}, f32[8,128]{1,0:T(8,128)}, u32[]{:S(2)}) copy-start(f32[8,128]{1,0:T(8,128)} %get-tuple-element.4) | copy-start | bytes 12292

commit v2 on v1

--- a/solution.py
+++ b/solution.py
@@ -31,7 +31,7 @@
 
 
 def kernel(
-    grid, unroll, lists, hardness, electroneg, gamma, geo,
+    grid, unroll, lists, hardness, electroneg, gamma, positions, types,
     charges, solution_ref,
     geo_halo, vec_halos, shares, features, lhs, weights, weight_col,
     current0, current1, eta_rows, gamma_rows, diagonal, image0, image1, blocks,
@@ -39,7 +39,7 @@
 ):
     tiles, nbr = lists.shape
     kinds = gamma.shape[0]
-    width = geo.shape[2]
+    width = types.shape[3] // tiles
     devices = math.prod(grid)
     scale = (tiles * width * VOLUME) ** (1.0 / 3.0) / CUTOFF
     me = [lax.axis_index(a) for a in AXES]
@@ -63,7 +63,6 @@
         d = lax.rem(my_id + j, devices)
         pl.semaphore_signal(barrier, inc=1, device_id=device_of(d), device_id_type=MESH)
 
-    pl.semaphore_wait(barrier, devices - 1)
 
     def halo_copy(buffer, send, recv, slot, o, where):
         return pltpu.make_async_remote_copy(
@@ -94,19 +93,25 @@
         return pltpu.make_async_remote_copy(
             src_ref=shares[k].at[0],
             dst_ref=shares[k].at[slot],
-            send_sem=sum_sends[k].at[j],
-            recv_sem=sum_recvs[k].at[slot],
+            send_sem=sum_sends[k],
+            recv_sem=sum_recvs[k],
             device_id=device_of(lax.rem(my_id + j, devices)),
             device_id_type=MESH,
         )
+
+    def wait_shares(k, sem):
+        rest = shares[k].at[pl.ds(1, devices - 1)]
+        pltpu.make_async_copy(rest, rest, sem).wait()
 
     def each_other(do):
         @pl.loop(1, devices)
         def _(j):
             do(j)
 
-    geo_halo[13] = geo[...]
-    start_halo(geo_halo, geo_send, geo_recv)
+    for u in range(tiles):
+        pair, top, span = u // 2, u % 2 * 4, slice(u * width, (u + 1) * width)
+        geo_halo[13, pair, top : top + 3, :] = positions[0, 0, 0, :, span]
+        geo_halo[13, pair, top + 3 : top + 4, :] = types[0, 0, :, span].astype(jnp.float32)
 
     row = lax.broadcasted_iota(jnp.int32, (8, width), 0)
     lane = lax.broadcasted_iota(jnp.int32, (1, width), 1)
@@ -155,6 +160,8 @@
                     eta_rows[pl.ds(u, 1), :] = eta8[r3 : r3 + 1]
                     gamma_rows[pl.ds(u, 1), :] = gammas[r3 : r3 + 1]
 
+    pl.semaphore_wait(barrier, devices - 1)
+    start_halo(geo_halo, geo_send, geo_recv)
     prepare(13, True)
 
     @pl.loop(0, 27)
@@ -267,7 +274,7 @@
 
             couple()
             q = [diag * w[s] + images[s][...] for s in systems]
-        each_other(lambda j: sum_copy(k, j, j).wait_recv())
+        wait_shares(k, sum_recvs[k])
         sums = jnp.sum(shares[k][...], axis=0)
         rr, rw, sr = [
             [jnp.sum(jnp.where(lane == i, sums[s : s + 1], 0.0), axis=1, keepdims=True) for s in systems]
@@ -293,15 +300,18 @@
             r = [r[s] - alpha[s] * along[s] for s in systems]
             w = [w[s] - alpha[s] * deep[s] for s in systems]
 
-    for s in systems:
-        solution_ref[s] = x[s]
-    charges[...] = x[0] - (sum_x[0] / sum_x[1]) * x[1]
+    charge = x[0] - (sum_x[0] / sum_x[1]) * x[1]
+    for u in range(tiles):
+        span = slice(u * width, (u + 1) * width)
+        charges[0, 0, :, span] = charge[u : u + 1]
+        for s in systems:
+            solution_ref[0, 0, 0, s : s + 1, span] = x[s][u : u + 1]
 
     end_send(geo_halo, geo_send, geo_recv)
     for k in range(ITERS - 1):
         end_send(vec_halos[k], vec_sends[k], vec_recvs[k])
     for k in range(ITERS):
-        each_other(lambda j: sum_copy(k, devices - j, j).wait_send())
+        wait_shares(k, sum_sends[k])
 
 
 def on_device(positions, types, tile_lists, hardness, electroneg, gamma_table):
@@ -310,25 +320,18 @@
     width = atoms // tiles
     grid = tuple(lax.axis_size(a) for a in AXES)
     devices = math.prod(grid)
-    unroll = next(u for u in (4, 3, 2, 1) if nbr % u == 0)
-    geo = jnp.concatenate(
-        [
-            jnp.transpose(positions.reshape(3, tiles, width), (1, 0, 2)),
-            types.reshape(tiles, 1, width).astype(jnp.float32),
-        ],
-        axis=1,
-    ).reshape(tiles // 2, 8, width)
+    unroll = next(u for u in (18, 16, 12, 8, 6, 4, 3, 2, 1) if nbr % u == 0)
     f32 = jnp.float32
     vmem = pl.BlockSpec(memory_space=pltpu.VMEM)
     smem = pl.BlockSpec(memory_space=pltpu.SMEM)
     rounds = ITERS - 1
-    charges, solution_ = pl.pallas_call(
+    return pl.pallas_call(
         functools.partial(kernel, grid, unroll),
         out_shape=(
-            jax.ShapeDtypeStruct((tiles, width), f32),
-            jax.ShapeDtypeStruct((2, tiles, width), f32),
+            jax.ShapeDtypeStruct((1, 1, 1, atoms), f32),
+            jax.ShapeDtypeStruct((1, 1, 1, 2, atoms), f32),
         ),
-        in_specs=[smem] * 4 + [vmem],
+        in_specs=[smem] * 4 + [vmem] * 2,
         out_specs=(vmem, vmem),
         scratch_shapes=[
             pltpu.VMEM((27, tiles // 2, 8, width), f32),
@@ -350,14 +353,13 @@
             pltpu.SemaphoreType.DMA((27,)),
             [pltpu.SemaphoreType.DMA((27,))] * rounds,
             [pltpu.SemaphoreType.DMA((27,))] * rounds,
-            [pltpu.SemaphoreType.DMA((devices,))] * ITERS,
-            [pltpu.SemaphoreType.DMA((devices,))] * ITERS,
+            [pltpu.SemaphoreType.DMA] * ITERS,
+            [pltpu.SemaphoreType.DMA] * ITERS,
         ],
         compiler_params=pltpu.CompilerParams(
             collective_id=0, has_side_effects=True, vmem_limit_bytes=56 * 2**20
         ),
-    )(tile_lists, hardness, electroneg, gamma_table, geo)
-    return charges.reshape(1, 1, 1, atoms), solution_.reshape(1, 1, 1, 2, atoms)
+    )(tile_lists, hardness, electroneg, gamma_table, positions, types)
 
 
 def solution(mesh):

time: 86.8 us -> 72.9 us (0.84)
  Pallas kernels: 81.9 us -> 68.8 us
  other arithmetic: 1.3 us -> 0 us
    pallas_call x1, Pallas kernels: 81.9 us -> 68.8 us  [on_device(): pl.pallas_call(functools.partial(kernel, grid, unroll), out_shape=(jax.Sh...]
    unnamed x3 -> x5, local copies, waits for them, and re-layouts: 0.6 us -> 3.19 us
    reshape x2 -> x0, local copies, waits for them, and re-layouts: 2.02 us -> none  [the longest x1 1.3 us: on_device(): solution_.reshape(1, 1, 1, 2, atoms)]
where the time goes in v2:
time: 72.9 us; the launch traced here: 72.6 us
  Pallas kernels  68.8 us (94%)
  local copies, waits for them, and re-layouts  3.19 us (4%)
    pallas_call x1, Pallas kernels, on_device(): pl.pallas_call(functools.partial(kernel, grid, unroll), out_shape=(jax.Sh...  68.8 us
    unnamed x5, local copies, waits for them, and re-layouts  3.19 us

profile of v2, /device:TPU:0, one launch (start us, length us, event | category | flops | bytes accessed | tf_op | source)
XLA Modules:
  0.0 72.6 jit_solution(13323438228158961593)
XLA Ops:
  0.6 1.3 %copy.8.positions = f32[1,1,1,3,1024]{4,3,2,1,0:T(4,128)} copy(f32[1,1,1,3,1024]{4,2,3,1,0:T(1,128)} %param.6) | data formatting | bytes 24576 | tf_op args[0]
  1.9 68.8 %shard_map.77 = (f32[1,1,1,1024]{3,2,1,0:T(1,128)}, f32[1,1,1,2,1024]{4,3,2,1,0:T(2,128)}) custom-call(s32[8,36]{1,0:T(8,128)} %lists.1, f32[4]{0:T(128)} %hardness.1, f32[4]{0:T(128)} %electroneg.1, f32[4]{0:T(128)} %gamma.1, f32[1,1,1,3,1024]{4,3,2,1,0:T(4,128)} %copy.8.positions, s32[1,1,1,1024]{3,2,1,0:T(1,128)} %types.1), custom_call_target="tpu_custom_call" | custom-call | tf_op jit(solution)/shard_map/pallas_call | solution.py:328
  70.7 0.0 copy-start
  70.7 1.3 %copy.11 = f32[1,1,1,1024]{3,2,1,0:T(1,128)} copy(f32[1,1,1,1024]{3,2,1,0:T(1,128)} %get-tuple-element.4) | data formatting | bytes 8192
  72.0 0.0 copy-done
  72.0 0.6 copy.12
Async XLA Ops:
  70.7 1.3 %copy-start = (f32[1,1,1,2,1024]{4,3,2,1,0:T(2,128)S(1)}, f32[1,1,1,2,1024]{4,3,2,1,0:T(2,128)}, u32[]{:S(2)}) copy-start(f32[1,1,1,2,1024]{4,3,2,1,0:T(2,128)} %get-tuple-element.5) | copy-start | bytes 24580

commit v3 on v2

--- a/solution.py
+++ b/solution.py
@@ -75,7 +75,7 @@
         )
 
     def each_neighbour(do):
-        @pl.loop(0, 27)
+        @pl.loop(0, 27, unroll=True)
         def _(o):
             where, there = neighbour(o)
 
@@ -260,7 +260,7 @@
             start_halo(buffer, send, recv)
         each_other(lambda j: sum_copy(k, devices - j, j).start())
         if not last:
-            @pl.loop(0, 27)
+            @pl.loop(0, 27, unroll=True)
             def _(o):
                 where, there = neighbour(o)
 

time: 72.9 us -> 67.9 us (0.931)
  Pallas kernels: 68.8 us -> 63.8 us
    pallas_call x1, Pallas kernels: 68.8 us -> 63.8 us  [on_device(): pl.pallas_call(functools.partial(kernel, grid, unroll), out_shape=(jax.Sh...]
where the time goes in v3:
time: 67.9 us; the launch traced here: 67.7 us
  Pallas kernels  63.8 us (94%)
  local copies, waits for them, and re-layouts  3.19 us (5%)
    pallas_call x1, Pallas kernels, on_device(): pl.pallas_call(functools.partial(kernel, grid, unroll), out_shape=(jax.Sh...  63.8 us
    unnamed x5, local copies, waits for them, and re-layouts  3.19 us

profile of v3, /device:TPU:0, one launch (start us, length us, event | category | flops | bytes accessed | tf_op | source)
XLA Modules:
  0.0 67.7 jit_solution(16181804871192561631)
XLA Ops:
  0.6 1.3 %copy.8.positions = f32[1,1,1,3,1024]{4,3,2,1,0:T(4,128)} copy(f32[1,1,1,3,1024]{4,2,3,1,0:T(1,128)} %param.6) | data formatting | bytes 24576 | tf_op args[0]
  1.9 63.8 %shard_map.77 = (f32[1,1,1,1024]{3,2,1,0:T(1,128)}, f32[1,1,1,2,1024]{4,3,2,1,0:T(2,128)}) custom-call(s32[8,36]{1,0:T(8,128)} %lists.1, f32[4]{0:T(128)} %hardness.1, f32[4]{0:T(128)} %electroneg.1, f32[4]{0:T(128)} %gamma.1, f32[1,1,1,3,1024]{4,3,2,1,0:T(4,128)} %copy.8.positions, s32[1,1,1,1024]{3,2,1,0:T(1,128)} %types.1), custom_call_target="tpu_custom_call" | custom-call | tf_op jit(solution)/shard_map/pallas_call | solution.py:328
  65.8 0.0 copy-start
  65.8 1.3 %copy.11 = f32[1,1,1,1024]{3,2,1,0:T(1,128)} copy(f32[1,1,1,1024]{3,2,1,0:T(1,128)} %get-tuple-element.4) | data formatting | bytes 8192
  67.1 0.0 copy-done
  67.1 0.6 copy.12
Async XLA Ops:
  65.8 1.3 %copy-start = (f32[1,1,1,2,1024]{4,3,2,1,0:T(2,128)S(1)}, f32[1,1,1,2,1024]{4,3,2,1,0:T(2,128)}, u32[]{:S(2)}) copy-start(f32[1,1,1,2,1024]{4,3,2,1,0:T(2,128)} %get-tuple-element.5) | copy-start | bytes 24580
